TPU v7x, 32 devices: a whole 2x2x4 slice. The times are simulated.
32 devices in a mesh: node: 2 (over x), row: 16 (over z, y, core).
Axes of the slice: x: 2, y: 2, z: 4, core: 2. Of those that a mesh axis runs over, the one named last changes fastest.
Arguments:
- hamiltonian: float32 [32, 7, 128, 128], P('row'), may hold values from -0.09375 to 0.09375
- column_blocks: int32 [32, 7], P('row'), may hold values from 0 to 31, as said below
- start_basis: float32 [4096, 256], P('row'), may hold values from -48 to 48
- node_re: float32 [6], P('node'), may hold values from 1.5 to 2.5
- node_im: float32 [6], P('node'), may hold values from 0.5 to 1.5
- weight_re: float32 [6], P('node'), may hold values from 0.5 to 1.5
- weight_im: float32 [6], P('node'), may hold values from -1 to 1
- sweep_count: int32 [6], P('node'), may hold values from 1 to 2, as said below
Outputs:
- basis: float32 [4096, 256], P('row')
Inputs may be any that keep to these rules, and one draw needn't show every extreme that they name: `column_blocks`: tile 0 of row block b lies in column block b, tile 1 in b - 2 and tile 2 in b + 2, taken cyclically modulo 32; every other tile lies within 2 blocks of b, cyclically. `sweep_count`: some node takes 1 sweep and some node takes 2.
All inputs are finite; a program needn't handle non-finite values.
Results may differ from a plain program's by a relative error of at most 0.00022.
Values sent between devices are 32-bit elements; how exact they have to be, the bound alone decides.
No kernel may reach another device: no remote copies, remote signals or barrier semaphores. Data moves between devices by JAX's collectives and lax.ppermute only.
A program may use at most 64 MiB of HBM per device.

v0:
```python
import math
import jax
import jax.numpy as jnp
from jax import lax
from jax.sharding import PartitionSpec as P

REACH = 2
SWEEPS = 2
NS_ITERS = 2


def extended_2(block, sides, width):
    for axis, dim in sides:
        count = lax.axis_size(axis)
        forward = [(i, i + 1) for i in range(count - 1)]
        forward.append((count - 1, 0))
        backward = [(target, source) for source, target in forward]
        low = lax.ppermute(
            lax.slice_in_dim(block, block.shape[dim] - width, None, axis=dim), axis, forward
        )
        high = lax.ppermute(lax.slice_in_dim(block, 0, width, axis=dim), axis, backward)
        block = jnp.concatenate([low, block, high], axis=dim)
    return block


def apply_local(hamiltonian, local_cols, extended):
    breadth = extended.shape[1]
    count_blocks = hamiltonian.shape[0]
    tile_rows = hamiltonian.shape[2]
    blocks = extended.reshape(-1, tile_rows, breadth)
    summed = jnp.zeros((count_blocks, tile_rows, breadth), jnp.float32)
    for column in range(hamiltonian.shape[1]):
        picked = jnp.take(blocks, local_cols[:, column], axis=0)
        summed = summed + jnp.einsum(
            "bij,bjw->biw", hamiltonian[:, column], picked, precision=lax.Precision.HIGHEST
        )
    return summed.reshape(count_blocks * tile_rows, breadth)


def local_gram(vectors):
    return lax.dot_general(
        vectors, vectors, (((0,), (0,)), ((), ())), precision=lax.Precision.HIGHEST
    )


def orthonormal(gram_matrix):
    norm_value = jnp.sqrt(jnp.sum(gram_matrix * gram_matrix) + 1e-06)
    matrix_a = gram_matrix / norm_value
    identity = jnp.eye(gram_matrix.shape[0], dtype=jnp.float32)
    current = identity
    for repeat in range(NS_ITERS):
        middle = 1.5 * identity - 0.5 * jnp.dot(current, matrix_a, precision=lax.Precision.HIGHEST)
        matrix_a = jnp.dot(matrix_a, middle, precision=lax.Precision.HIGHEST)
        current = jnp.dot(middle, current, precision=lax.Precision.HIGHEST)
    return (current, norm_value)


def finish(vectors, gram_matrix, row_scale):
    mixing, norm_value = orthonormal(gram_matrix)
    return (
        row_scale * jnp.dot(vectors, mixing, precision=lax.Precision.HIGHEST) / jnp.sqrt(norm_value)
    )


def on_device(
    hamiltonian, column_blocks, start_basis, node_re, node_im, weight_re, weight_im, sweep_count
):
    count_blocks = hamiltonian.shape[0]
    tile_rows = hamiltonian.shape[2]
    devices_row = lax.axis_size("row")
    first_block = lax.axis_index("row") * count_blocks
    local_cols = (column_blocks - first_block + REACH + count_blocks * devices_row) % (
        count_blocks * devices_row
    )
    rim_rows = REACH * tile_rows
    row_scale = math.sqrt(start_basis.shape[0] * devices_row)
    modulus = node_re * node_re + node_im * node_im
    inverse_re = node_re / modulus
    inverse_im = -node_im / modulus
    power_re, power_im = (inverse_re, inverse_im)
    listed = []
    for degree in range(SWEEPS + 1):
        active = (sweep_count >= degree).astype(jnp.float32)
        listed.append(jnp.sum(active * (weight_re * power_re - weight_im * power_im)))
        power_re, power_im = (
            power_re * inverse_re - power_im * inverse_im,
            power_re * inverse_im + power_im * inverse_re,
        )
    coefficients = lax.psum(jnp.stack(listed), "node")
    krylov = start_basis
    filtered = coefficients[0] * start_basis
    for degree in range(1, SWEEPS + 1):
        extended = extended_2(krylov, (("row", 0),), rim_rows)
        krylov = apply_local(hamiltonian, local_cols, extended)
        filtered = filtered + coefficients[degree] * krylov
    gram_matrix = lax.psum(local_gram(filtered), "row")
    return finish(filtered, gram_matrix, row_scale)


def solution(mesh):
    return jax.shard_map(
        on_device,
        mesh=mesh,
        in_specs=(
            P("row", None, None, None),
            P("row", None),
            P("row", None),
            P("node"),
            P("node"),
            P("node"),
            P("node"),
            P("node"),
        ),
        out_specs=P("row", None),
        check_vma=False,
    )
```

profile of v0, /device:TPU:1, one launch (start us, length us, event | category | flops | bytes accessed | tf_op | source)
XLA Modules:
  0.0 155.2 jit_solution(14468664168108451764)
XLA Ops:
  6.5 2.6 %collective-permute-start = (f32[256,256]{1,0:T(8,128)}, f32[256,256]{1,0:T(8,128)S(1)}, u32[]{:S(2)}, u32[]{:S(2)}) collective-permute-start(f32[256,256]{1,0:T(8,128)} %param.12), channel_id=1, source_target_pairs={{0,1},{1,2},{2,3},{3,4},{4,5},{5,6},{6,7},{7,8},{8,9},{9,10},{10,1... | collective-permute-start | bytes 786440 | tf_op jit(solution)/shard_map/ppermute | solution.py:18
  9.2 0.7 copy-done.20
  10.7 0.6 compare_and_fusion.4
  11.3 0.6 compare_and_fusion.2
  12.4 0.6 compare_and_fusion
  13.1 0.6 pad_clamp_fusion.1
  13.7 0.6 pad_clamp_fusion
  14.9 3.1 %collective-permute-done.1 = f32[256,256]{1,0:T(8,128)S(1)} collective-permute-done((f32[256,256]{1,0:T(8,128)}, f32[256,256]{1,0:T(8,128)S(1)}, u32[]{:S(2)}, u32[]{:S(2)}) %collective-permute-start.1) | collective-permute-done | bytes 262176 | tf_op jit(solution)/shard_map/ppermute | solution.py:21
  18.0 1.0 pad_maximum_fusion
  21.9 0.7 gather_fusion.5
  22.6 0.7 gather_fusion.6
  23.3 1.1 fusion.18
  24.4 0.6 copy-done.9
  25.4 0.7 copy-done.5
  26.6 0.6 copy-done.11
  27.7 0.7 copy-done.7
  30.7 0.6 copy-done.17
  31.4 0.6 fusion.79
  32.0 1.9 %pad_maximum_fusion.2 = f32[3]{0:T(128)S(1)} fusion(f32[1]{0:T(128)} %bitcast.2, f32[1]{0:T(128)} %bitcast.1, f32[1]{0:T(128)} %bitcast), kind=kLoop, calls=%fused_computation.151 | loop fusion | flops 6 | bytes 24 | tf_op jit(solution)/shard_map/stack | solution.py:89
  33.9 4.1 %psum.14 = f32[3]{0:T(128)S(1)} all-reduce(f32[3]{0:T(128)S(1)} %pad_maximum_fusion.2), channel_id=1, replica_groups=mesh['node'=2,'row'=16] {'node'}, use_global_device_ids=true, to_apply=%region_3.4 | all-reduce | flops 3 | bytes 24 | tf_op jit(solution)/shard_map/psum | solution.py:89
  38.0 0.6 fusion.97
  40.1 0.6 gather_fusion.9
  40.6 0.6 gather_fusion.10
  41.2 0.7 gather_fusion.11
  41.9 0.7 gather_fusion.12
  42.6 1.4 gather_fusion.13
  48.4 1.1 fusion.3
  49.5 1.3 bitcast_add_fusion
  50.8 1.3 fusion.98
  52.1 91.0 %all-reduce.2.cloned.1.call-done = f32[256,256]{1,0:T(8,128)} async-done(((f32[256,256]{1,0:T(8,128)}), f32[256,256]{1,0:T(8,128)}) %all-reduce.2.cloned.1.call-update) | async-done | bytes 262160 | tf_op jit(solution)/shard_map/psum | solution.py:96
  143.1 1.7 %multiply_reduce_fusion = f32[]{:T(128)} fusion(f32[256,256]{1,0:T(8,128)} %all-reduce.2.cloned.1.call-done), kind=kLoop, calls=%fused_computation.52 | loop fusion | flops 131071 | bytes 262148 | tf_op jit(solution)/shard_map/reduce_sum | solution.py:47
  147.3 1.1 fusion
  (93 shorter events, 16.2 us)
Async XLA Ops:
  6.5 136.6 %all-reduce.2.cloned.1.call-start = ((), (), s32[]{:S(2)}) async-start(), calls=%async_computation | async-start | bytes 524288 | tf_op jit(solution)/shard_map/psum | solution.py:96
  6.5 8.3 %collective-permute-start = (f32[256,256]{1,0:T(8,128)}, f32[256,256]{1,0:T(8,128)S(1)}, u32[]{:S(2)}, u32[]{:S(2)}) collective-permute-start(f32[256,256]{1,0:T(8,128)} %param.12), channel_id=1, source_target_pairs={{0,1},{1,2},{2,3},{3,4},{4,5},{5,6},{6,7},{7,8},{8,9},{9,10},{10,1... | collective-permute-start | bytes 786440 | tf_op jit(solution)/shard_map/ppermute | solution.py:18
  9.2 8.8 %collective-permute-start.1 = (f32[256,256]{1,0:T(8,128)}, f32[256,256]{1,0:T(8,128)S(1)}, u32[]{:S(2)}, u32[]{:S(2)}) collective-permute-start(f32[256,256]{1,0:T(8,128)} %param.12), channel_id=1, source_target_pairs={{1,0},{2,1},{3,2},{4,3},{5,4},{6,5},{7,6},{8,7},{9,8},{10,9},{11,1... | collective-permute-start | bytes 786440 | tf_op jit(solution)/shard_map/ppermute | solution.py:21
  9.2 0.7 copy-start.20
  13.1 8.2 %copy-start.4 = (s32[1024]{0:T(1024)}, s32[1024]{0:T(1024)S(1)}, u32[]{:S(2)}) copy-start(s32[1024]{0:T(1024)S(1)} %pad_clamp_fusion.2) | copy-start | bytes 12292
  13.7 0.7 copy-start.21
  13.7 0.7 copy-start.22
  21.3 2.0 %copy-start = (f32[2,7,128,128]{3,2,1,0:T(8,128)S(1)}, f32[2,7,128,128]{3,2,1,0:T(8,128)}, u32[]{:S(2)}) copy-start(f32[2,7,128,128]{3,2,1,0:T(8,128)} %param.10) | copy-start | bytes 2752516
  24.3 0.6 copy-start.9
  25.4 0.7 copy-start.5
  26.6 0.7 copy-start.11
  27.7 0.7 copy-start.7
  28.4 0.6 copy-start.13
  29.0 0.7 copy-start.15
  29.7 1.0 copy-start.24
  29.7 1.1 copy-start.25
  30.1 8.5 %collective-permute-start.2 = (f32[256,256]{1,0:T(8,128)S(1)}, f32[256,256]{1,0:T(8,128)S(1)}, u32[]{:S(2)}, u32[]{:S(2)}) collective-permute-start(f32[256,256]{1,0:T(8,128)S(1)} %bitcast.89), channel_id=1, source_target_pairs={{0,1},{1,2},{2,3},{3,4},{4,5},{5,6},{6,7},{7,8},{8,9},{9,10},{10,1... | collective-permute-start | bytes 786440 | tf_op jit(solution)/shard_map/ppermute | solution.py:18
  30.2 8.7 %collective-permute-start.3 = (f32[256,256]{1,0:T(8,128)S(1)}, f32[256,256]{1,0:T(8,128)S(1)}, u32[]{:S(2)}, u32[]{:S(2)}) collective-permute-start(f32[256,256]{1,0:T(8,128)S(1)} %bitcast.90), channel_id=1, source_target_pairs={{1,0},{2,1},{3,2},{4,3},{5,4},{6,5},{7,6},{8,7},{9,8},{10,9},{11,1... | collective-permute-start | bytes 786440 | tf_op jit(solution)/shard_map/ppermute | solution.py:21
  30.7 0.6 copy-start.17
  30.7 0.6 copy-start.18
  30.7 0.7 copy-start.23
  42.6 1.4 copy-start.19
  44.0 0.6 copy-start.10
  44.6 0.7 copy-start.6
  45.3 0.7 copy-start.12
  45.9 0.7 copy-start.8
  46.6 0.6 copy-start.14
  47.2 0.9 copy-start.2
  47.7 0.7 copy-start.16
  48.4 1.1 copy-start.1
  143.1 2.4 %copy-start.3 = (f32[256,256]{1,0:T(8,128)S(1)}, f32[256,256]{1,0:T(8,128)}, u32[]{:S(2)}) copy-start(f32[256,256]{1,0:T(8,128)} %all-reduce.2.cloned.1.call-done) | copy-start | bytes 786436
Sparse Core Ops, SparseCore 0:
  52.2 90.7 all-reduce.1
where the time goes:
time: 156 us; the launch traced here: 155 us
  waiting for transfers between devices  94.3 us (60%)
  local copies, waits for them, and re-layouts  16 us (10%)
  between operations  14.6 us (9%)
  matrix products  11.9 us (8%)
  other arithmetic  11.2 us (7%)
  blocking collectives  4.06 us (3%)
  starting transfers between devices  3.19 us (2%)
    psum x1, waiting for transfers between devices, on_device(): gram_matrix = lax.psum(local_gram(filtered), 'row')  91 us
    gather x14, local copies, waits for them, and re-layouts, apply_local(): picked = jnp.take(blocks, local_cols[:, column], axis=0)  9.23 us
    dot_general x14, matrix products, apply_local(): jnp.einsum('bij,bjw->biw', hamiltonian[:, column], picked, precision=lax....  7.73 us
    unnamed x52, local copies, waits for them, and re-layouts  5.86 us
    psum x1, blocking collectives, on_device(): coefficients = lax.psum(jnp.stack(listed), 'node')  4.06 us
    ppermute x2, waiting for transfers between devices, extended_2(): lax.ppermute(lax.slice_in_dim(block, 0, width, axis=dim), axis, backward)  3.36 us
  transfers between devices with their start and end apart: 5, of which 3 were waited for; matrix products, arithmetic and copies ran while one was open for 5% of the time, Pallas kernels for 0%

commit v1 on v0

--- a/solution.py
+++ b/solution.py
@@ -93,7 +93,8 @@
         extended = extended_2(krylov, (("row", 0),), rim_rows)
         krylov = apply_local(hamiltonian, local_cols, extended)
         filtered = filtered + coefficients[degree] * krylov
-    gram_matrix = lax.psum(local_gram(filtered), "row")
+    original = local_gram(filtered)
+    gram_matrix = jax.lax.all_gather(original, axis_name="row").sum(axis=0)
     return finish(filtered, gram_matrix, row_scale)
 
 

time: 156 us -> 122 us (0.78)
  waiting for transfers between devices: 94.3 us -> 56.4 us
  matrix products: 11.9 us -> 19 us
  local copies, waits for them, and re-layouts: 16 us -> 9.99 us
  other arithmetic: 11.2 us -> 13 us
    psum x1 -> x0, waiting for transfers between devices: 91 us -> none  [on_device(): gram_matrix = lax.psum(local_gram(filtered), 'row')]
    all_gather x0 -> x1, waiting for transfers between devices: none -> 52.8 us  [on_device(): gram_matrix = jax.lax.all_gather(original, axis_name='row').sum(axis=0)]
    dot_general x14, matrix products: 7.73 us -> 14.8 us  [apply_local(): jnp.einsum('bij,bjw->biw', hamiltonian[:, column], picked, precision=lax....]
    unnamed x52 -> x26, local copies, waits for them, and re-layouts: 5.86 us -> 0.07 us
    reduce_sum x0 -> x1, other arithmetic: none -> 2.48 us  [on_device(): gram_matrix = jax.lax.all_gather(original, axis_name='row').sum(axis=0)]
    ppermute x2, starting transfers between devices: 2.69 us -> 4.36 us  [extended_2(): lax.ppermute(lax.slice_in_dim(block, block.shape[dim] - width, None, axis...]
  transfers between devices with their start and end apart: 5 -> 5, of which waited for: 3 -> 2; matrix products, arithmetic and copies ran while one was open for 5% -> 7% of each run, Pallas kernels for 0% -> 0%
where the time goes in v1:
time: 122 us; the launch traced here: 121 us
  waiting for transfers between devices  56.4 us (46%)
  matrix products  19 us (16%)
  between operations  14.6 us (12%)
  other arithmetic  13 us (11%)
  local copies, waits for them, and re-layouts  9.99 us (8%)
  starting transfers between devices  4.42 us (4%)
  blocking collectives  4.06 us (3%)
    all_gather x1, waiting for transfers between devices, on_device(): gram_matrix = jax.lax.all_gather(original, axis_name='row').sum(axis=0)  52.8 us
    dot_general x14, matrix products, apply_local(): jnp.einsum('bij,bjw->biw', hamiltonian[:, column], picked, precision=lax....  14.8 us
    gather x14, local copies, waits for them, and re-layouts, apply_local(): picked = jnp.take(blocks, local_cols[:, column], axis=0)  8.98 us
    ppermute x2, starting transfers between devices, extended_2(): lax.ppermute(lax.slice_in_dim(block, block.shape[dim] - width, None, axis...  4.36 us
    psum x1, blocking collectives, on_device(): coefficients = lax.psum(jnp.stack(listed), 'node')  4.06 us
    ppermute x2, waiting for transfers between devices, extended_2(): lax.ppermute(lax.slice_in_dim(block, 0, width, axis=dim), axis, backward)  3.6 us
    and x5, other arithmetic, apply_local(): picked = jnp.take(blocks, local_cols[:, column], axis=0)  2.85 us
    reduce_sum x1, other arithmetic, on_device(): gram_matrix = jax.lax.all_gather(original, axis_name='row').sum(axis=0)  2.48 us
  transfers between devices with their start and end apart: 5, of which 2 were waited for; matrix products, arithmetic and copies ran while one was open for 7% of the time, Pallas kernels for 0%

profile of v1, /device:TPU:1, one launch (start us, length us, event | category | flops | bytes accessed | tf_op | source)
XLA Modules:
  0.0 121.5 jit_solution(4901674898355003)
XLA Ops:
  6.5 2.6 %collective-permute-start = (f32[256,256]{1,0:T(8,128)}, f32[256,256]{1,0:T(8,128)S(1)}, u32[]{:S(2)}, u32[]{:S(2)}) collective-permute-start(f32[256,256]{1,0:T(8,128)} %param.12), channel_id=1, source_target_pairs={{0,1},{1,2},{2,3},{3,4},{4,5},{5,6},{6,7},{7,8},{8,9},{9,10},{10,1... | collective-permute-start | bytes 786440 | tf_op jit(solution)/shard_map/ppermute | solution.py:18
  9.2 0.7 and_select_fusion
  11.3 0.6 compare_and_fusion.6
  13.1 1.2 %fusion.82 = (f32[3]{0:T(128)}, f32[3]{0:T(128)}) fusion(f32[3]{0:T(128)} %param.13, f32[3]{0:T(128)} %param.14), kind=kLoop, calls=%fused_computation.156 | loop fusion | flops 18 | bytes 48 | tf_op jit(solution)/shard_map/div | solution.py:78
  14.4 3.6 %collective-permute-done.1 = f32[256,256]{1,0:T(8,128)S(1)} collective-permute-done((f32[256,256]{1,0:T(8,128)}, f32[256,256]{1,0:T(8,128)S(1)}, u32[]{:S(2)}, u32[]{:S(2)}) %collective-permute-start.1) | collective-permute-done | bytes 262176 | tf_op jit(solution)/shard_map/ppermute | solution.py:21
  18.0 1.0 pad_maximum_fusion
  23.1 1.2 fusion.18
  24.3 1.1 convolution_add_fusion.11
  25.4 1.1 convolution_add_fusion.10
  26.5 1.1 convolution_add_fusion.9
  27.6 1.1 convolution_add_fusion.8
  29.7 1.7 %collective-permute-start.2 = (f32[256,256]{1,0:T(8,128)S(1)}, f32[256,256]{1,0:T(8,128)S(1)}, u32[]{:S(2)}, u32[]{:S(2)}) collective-permute-start(f32[256,256]{1,0:T(8,128)S(1)} %bitcast.92), channel_id=1, source_target_pairs={{0,1},{1,2},{2,3},{3,4},{4,5},{5,6},{6,7},{7,8},{8,9},{9,10},{10,1... | collective-permute-start | bytes 786440 | tf_op jit(solution)/shard_map/ppermute | solution.py:18
  31.5 0.7 fusion.79
  32.1 2.0 %pad_maximum_fusion.2 = f32[3]{0:T(128)S(1)} fusion(f32[1]{0:T(128)} %bitcast.2, f32[1]{0:T(128)} %bitcast.1, f32[1]{0:T(128)} %bitcast), kind=kLoop, calls=%fused_computation.151 | loop fusion | flops 6 | bytes 24 | tf_op jit(solution)/shard_map/stack | solution.py:89
  34.1 4.1 %psum.7 = f32[3]{0:T(128)S(1)} all-reduce(f32[3]{0:T(128)S(1)} %pad_maximum_fusion.2), channel_id=1, replica_groups=mesh['node'=2,'row'=16] {'node'}, use_global_device_ids=true, to_apply=%region_3.4 | all-reduce | flops 3 | bytes 24 | tf_op jit(solution)/shard_map/psum | solution.py:89
  38.2 0.7 fusion.97
  38.9 1.4 %gather_fusion.13 = f32[2,128,256]{2,1,0:T(8,128)} fusion(f32[6,128,256]{2,1,0:T(8,128)S(1)} %bitcast.76, s32[1024]{0:T(1024)} %copy-done.3), kind=kCustom, calls=%fused_computation.13.clone | custom fusion | bytes 524296 | tf_op jit(solution)/shard_map/jit(_take)/gather | solution.py:33
  40.3 0.7 gather_fusion.12
  41.5 0.7 gather_fusion.10
  44.0 1.2 fusion.10
  45.2 1.1 convolution_add_fusion.5
  46.3 1.1 convolution_add_fusion.4
  47.4 1.1 convolution_add_fusion.3
  48.5 1.1 convolution_add_fusion.2
  49.5 1.1 convolution_add_fusion.1
  50.7 1.8 %fusion.3 = f32[2,256,128]{1,2,0:T(8,128)S(1)} fusion(f32[2,256,128]{1,2,0:T(8,128)S(1)} %convolution_add_fusion.1, f32[2,128,256]{2,1,0:T(8,128)S(1)} %copy-done.2, f32[]{:T(128)} %bitcast.15, pred[2]{0:T(512)(128)(4,1)} %compare_and_fusion, f32[2,7,128,128]{3,2,1,0:T(8,128)S(1)} %copy-done), kind=kOutput, calls=%fused_computation.21 | convolution fusion | flops 100859904 | bytes 917510 | tf_op jit(solution)/shard_map/bij,bjw->biw/dot_general | solution.py:34
  52.5 1.3 %bitcast_add_fusion = f32[256,256]{1,0:T(8,128)S(1)} fusion(f32[2,256,128]{1,2,0:T(8,128)S(1)} %fusion.3, f32[256,256]{1,0:T(8,128)S(1)} %copy-done.1, f32[]{:T(128)} %bitcast.4, f32[]{:T(128)} %bitcast.3, f32[2,256,128]{1,2,0:T(8,128)S(1)} %convolution_add_fusion.6), kind=kLoop, calls=%fused_computation.35 | loop fusion | flops 262144 | bytes 1048584 | tf_op jit(solution)/shard_map/add | solution.py:95
  53.8 1.3 %fusion.98 = f32[256,256]{1,0:T(8,128)} fusion(f32[256,256]{1,0:T(8,128)S(1)} %bitcast_add_fusion), kind=kOutput, calls=%fused_computation.172 | convolution fusion | flops 201326592 | bytes 524288 | tf_op jit(solution)/shard_map/dot_general | solution.py:41
  55.1 52.8 %all-gather.3.cloned.1.call-done = f32[4096,256]{1,0:T(8,128)} async-done(((f32[256,256]{1,0:T(8,128)}), f32[4096,256]{1,0:T(8,128)}) %all-gather.3.cloned.1.call-update) | async-done | bytes 4194320 | tf_op jit(solution)/shard_map/all_gather | solution.py:97
  107.9 2.5 %reduce_sum.48 = f32[256,256]{1,0:T(8,128)S(1)} reduce(f32[16,256,256]{2,1,0:T(8,128)} %bitcast.90, f32[]{:T(128)} %constant.22.clone.1), dimensions={0}, to_apply=%region_4.6 | reduce | flops 983040 | bytes 4456452 | tf_op jit(solution)/shard_map/reduce_sum | solution.py:97
  110.4 0.7 multiply_reduce_fusion
  113.5 1.1 fusion
  (68 shorter events, 11.7 us)
Async XLA Ops:
  6.5 16.5 %copy-start = (f32[2,7,128,128]{3,2,1,0:T(8,128)S(1)}, f32[2,7,128,128]{3,2,1,0:T(8,128)}, u32[]{:S(2)}) copy-start(f32[2,7,128,128]{3,2,1,0:T(8,128)} %param.10) | copy-start | bytes 2752516
  6.5 101.4 %all-gather.3.cloned.1.call-start = ((), (), s32[]{:S(2)}) async-start(), calls=%async_computation | async-start | bytes 4456448 | tf_op jit(solution)/shard_map/all_gather | solution.py:97
  6.5 7.9 %collective-permute-start = (f32[256,256]{1,0:T(8,128)}, f32[256,256]{1,0:T(8,128)S(1)}, u32[]{:S(2)}, u32[]{:S(2)}) collective-permute-start(f32[256,256]{1,0:T(8,128)} %param.12), channel_id=1, source_target_pairs={{0,1},{1,2},{2,3},{3,4},{4,5},{5,6},{6,7},{7,8},{8,9},{9,10},{10,1... | collective-permute-start | bytes 786440 | tf_op jit(solution)/shard_map/ppermute | solution.py:18
  9.2 8.8 %collective-permute-start.1 = (f32[256,256]{1,0:T(8,128)}, f32[256,256]{1,0:T(8,128)S(1)}, u32[]{:S(2)}, u32[]{:S(2)}) collective-permute-start(f32[256,256]{1,0:T(8,128)} %param.12), channel_id=1, source_target_pairs={{1,0},{2,1},{3,2},{4,3},{5,4},{6,5},{7,6},{8,7},{9,8},{10,9},{11,1... | collective-permute-start | bytes 786440 | tf_op jit(solution)/shard_map/ppermute | solution.py:21
  13.1 6.5 %copy-start.3 = (s32[1024]{0:T(1024)}, s32[1024]{0:T(1024)S(1)}, u32[]{:S(2)}) copy-start(s32[1024]{0:T(1024)S(1)} %pad_clamp_fusion) | copy-start | bytes 12292
  13.1 7.6 %copy-start.4 = (s32[1024]{0:T(1024)}, s32[1024]{0:T(1024)S(1)}, u32[]{:S(2)}) copy-start(s32[1024]{0:T(1024)S(1)} %pad_clamp_fusion.3) | copy-start | bytes 12292
  13.1 6.4 %copy-start.5 = (s32[1024]{0:T(1024)}, s32[1024]{0:T(1024)S(1)}, u32[]{:S(2)}) copy-start(s32[1024]{0:T(1024)S(1)} %pad_clamp_fusion.1) | copy-start | bytes 12292
  23.0 5.6 %copy-start.7 = (pred[2]{0:T(512)(128)(4,1)S(1)}, pred[2]{0:T(512)(128)(4,1)}, u32[]{:S(2)}) copy-start(pred[2]{0:T(512)(128)(4,1)} %compare_and_fusion.1) | copy-start | bytes 10
  23.1 6.1 %copy-start.6 = (pred[2]{0:T(512)(128)(4,1)S(1)}, pred[2]{0:T(512)(128)(4,1)}, u32[]{:S(2)}) copy-start(pred[2]{0:T(512)(128)(4,1)} %compare_and_fusion) | copy-start | bytes 10
  23.1 8.4 %copy-start.8 = (f32[3]{0:T(128)S(1)}, f32[3]{0:T(128)}, u32[]{:S(2)}) copy-start(f32[3]{0:T(128)} %get-tuple-element.16) | copy-start | bytes 40
  23.1 8.4 %copy-start.9 = (f32[3]{0:T(128)S(1)}, f32[3]{0:T(128)}, u32[]{:S(2)}) copy-start(f32[3]{0:T(128)} %get-tuple-element.17) | copy-start | bytes 40
  23.1 8.3 %copy-start.10 = (s32[3]{0:T(128)S(1)}, s32[3]{0:T(128)}, u32[]{:S(2)}) copy-start(s32[3]{0:T(128)} %param.17) | copy-start | bytes 40
  23.1 8.3 %copy-start.11 = (f32[3]{0:T(128)S(1)}, f32[3]{0:T(128)}, u32[]{:S(2)}) copy-start(f32[3]{0:T(128)} %param.16) | copy-start | bytes 40
  23.1 8.3 %copy-start.12 = (f32[3]{0:T(128)S(1)}, f32[3]{0:T(128)}, u32[]{:S(2)}) copy-start(f32[3]{0:T(128)} %param.15) | copy-start | bytes 40
  29.6 9.2 %collective-permute-start.3 = (f32[256,256]{1,0:T(8,128)S(1)}, f32[256,256]{1,0:T(8,128)S(1)}, u32[]{:S(2)}, u32[]{:S(2)}) collective-permute-start(f32[256,256]{1,0:T(8,128)S(1)} %bitcast.91), channel_id=1, source_target_pairs={{1,0},{2,1},{3,2},{4,3},{5,4},{6,5},{7,6},{8,7},{9,8},{10,9},{11,1... | collective-permute-start | bytes 786440 | tf_op jit(solution)/shard_map/ppermute | solution.py:21
  29.7 9.1 %collective-permute-start.2 = (f32[256,256]{1,0:T(8,128)S(1)}, f32[256,256]{1,0:T(8,128)S(1)}, u32[]{:S(2)}, u32[]{:S(2)}) collective-permute-start(f32[256,256]{1,0:T(8,128)S(1)} %bitcast.92), channel_id=1, source_target_pairs={{0,1},{1,2},{2,3},{3,4},{4,5},{5,6},{6,7},{7,8},{8,9},{9,10},{10,1... | collective-permute-start | bytes 786440 | tf_op jit(solution)/shard_map/ppermute | solution.py:18
  43.9 6.7 %copy-start.2 = (f32[2,128,256]{2,1,0:T(8,128)S(1)}, f32[2,128,256]{2,1,0:T(8,128)}, u32[]{:S(2)}) copy-start(f32[2,128,256]{2,1,0:T(8,128)} %gather_fusion.13) | copy-start | bytes 786436
  44.0 8.5 %copy-start.1 = (f32[256,256]{1,0:T(8,128)S(1)}, f32[256,256]{1,0:T(8,128)}, u32[]{:S(2)}) copy-start(f32[256,256]{1,0:T(8,128)} %param.12) | copy-start | bytes 786436
Sparse Core Ops, SparseCore 0:
  55.2 52.6 all-gather.2
